TPU v7x, 32 devices: a whole 2x2x4 slice. The times are simulated.
32 devices in a mesh: wide: 8 (over y, x, core), narrow: 4 (over z).
Axes of the slice: x: 2, y: 2, z: 4, core: 2. Of those that a mesh axis runs over, the one named last changes fastest.
Arguments:
- hidden_in: bfloat16 [32, 512, 1024], P(('wide', 'narrow')), may hold values from -6 to 6
- memory: bfloat16 [32, 2, 588, 1024], P(('wide', 'narrow')), may hold values from -6 to 6
- segment_ids: int32 [32, 512], P(('wide', 'narrow')), may hold values from 0 to 3, never falling along the last dimension, each value on 1 to 256 neighbouring positions
- image_ids: int32 [32, 4], P(('wide', 'narrow')), may hold values from 0 to 1
- attn_in: bfloat16 [6, 1024, 1024], P(None, 'narrow'), may hold values from -0.1875 to 0.1875
- attn_out: bfloat16 [2, 1024, 1024], P(None, 'narrow'), may hold values from -1.5 to 1.5
- mlp_in: bfloat16 [1024, 4096], P('narrow'), may hold values from -0.1875 to 0.1875
- mlp_out: bfloat16 [4096, 1024], P('narrow'), may hold values from -0.09375 to 0.09375
- gains: bfloat16 [3, 1024], P(None, 'narrow'), may hold values from 0.5 to 1.5
- shifts: bfloat16 [10, 1024], P(None, 'narrow'), may hold values from -3 to 3
- mlp_bias: bfloat16 [4096], P('narrow'), may hold values from -3 to 3
- cotangent: bfloat16 [32, 512, 1024], P(('wide', 'narrow')), may hold values from -6 to 6
Outputs:
- layer_out: bfloat16 [32, 512, 1024], P(('wide', 'narrow'))
- grad_input: float32 [32, 512, 1024], P(('wide', 'narrow'))
- grad_memory: float32 [32, 2, 588, 1024], P(('wide', 'narrow'))
- grad_attn_in: float32 [6, 1024, 1024], P(None, 'narrow')
- grad_attn_out: float32 [2, 1024, 1024], P(None, 'narrow')
- grad_mlp_in: float32 [1024, 4096], P('narrow')
- grad_mlp_out: float32 [4096, 1024], P('narrow')
- grad_gains: float32 [3, 1024], P(None, 'narrow')
- grad_shifts: float32 [10, 1024], P(None, 'narrow')
- grad_mlp_bias: float32 [4096], P('narrow')
Inputs may be any that keep to these rules, and one draw needn't show every extreme that they name: `segment_ids`: in each row the page id never falls; each of the 4 pages holds 1 to 256 tokens, and one holds exactly 256.
All inputs are finite; a program needn't handle non-finite values.
Results may differ from a plain program's by a relative error of at most 0.017.
Values may be sent and summed in bfloat16 or wider, within the bound.
A program may use at most 384 MiB of HBM per device.

v0:
```python
import jax
import jax.numpy as jnp
from jax import lax
from jax.sharding import PartitionSpec as P

HEADS = 16


norm_eps = 1e-05
masked_score = -1e30


def layer_norm(values, gain, shift):
    centered = values - jnp.mean(values, axis=-1, keepdims=True)
    variance = jnp.mean(centered * centered, axis=-1, keepdims=True)
    return centered * lax.rsqrt(variance + norm_eps) * gain + shift


def gelu_exact(values):
    return jax.nn.gelu(values, approximate=False)


def matmul(left, right):
    return jnp.dot(left, right, preferred_element_type=jnp.float32)


def left_grad(left, right):
    return jnp.einsum("ra,rb->ab", left, right, preferred_element_type=jnp.float32)


def right_grad(grad, weight):
    return jnp.einsum("rb,ab->ra", grad, weight, preferred_element_type=jnp.float32)


def split_heads(values, heads):
    return values.reshape(values.shape[0], heads, values.shape[1] // heads)


def self_mask(segments):

    def allowed(start, block):
        query_pos = start + lax.iota(jnp.int32, block)
        key_pos = lax.iota(jnp.int32, segments.shape[0])
        return (segments[:, None] == segments[None, :]) & (key_pos[None, :] <= query_pos[:, None])

    return allowed


def cross_mask(token_image, key_image):

    def allowed(start, block):
        return token_image[:, None] == key_image[None, :]

    return allowed


def attention_forward(queries, keys_all, values_all, allowed, block):

    def one_block(block_index):
        start = block_index * block
        scores = jnp.einsum("qhe,khe->hqk", queries, keys_all, preferred_element_type=jnp.float32)
        scores = jnp.where(allowed(start, block)[None], scores, masked_score)
        top = jnp.max(scores, axis=-1, keepdims=True)
        expo = jnp.exp(scores - top)
        total = jnp.sum(expo, axis=-1, keepdims=True)
        probs = (expo / total).astype(jnp.bfloat16)
        mixed = jnp.einsum("hqk,khe->qhe", probs, values_all, preferred_element_type=jnp.float32)
        return (mixed.astype(jnp.bfloat16), (top + jnp.log(total))[..., 0])

    count = queries.shape[0] // block
    mixed, log_total = lax.map(one_block, lax.iota(jnp.int32, count))
    return (mixed.reshape(queries.shape), log_total)


def attention_backward(queries, keys_all, values_all, grad_mixed, log_total, allowed, block):

    def one_block(carry, block_index):
        acc_keys, acc_values = carry
        start = block_index * block
        scores = jnp.einsum("qhe,khe->hqk", queries, keys_all, preferred_element_type=jnp.float32)
        scores = jnp.where(allowed(start, block)[None], scores, masked_score)
        probs = jnp.exp(scores - log_total[block_index][..., None])
        acc_values = acc_values + jnp.einsum(
            "hqk,qhe->khe",
            probs.astype(jnp.bfloat16),
            grad_mixed,
            preferred_element_type=jnp.float32,
        )
        grad_probs = jnp.einsum(
            "qhe,khe->hqk", grad_mixed, values_all, preferred_element_type=jnp.float32
        )
        inner = jnp.sum(probs * grad_probs, axis=-1, keepdims=True)
        grad_scores = (probs * (grad_probs - inner)).astype(jnp.bfloat16)
        grad_query = jnp.einsum(
            "hqk,khe->qhe", grad_scores, keys_all, preferred_element_type=jnp.float32
        )
        acc_keys = acc_keys + jnp.einsum(
            "hqk,qhe->khe", grad_scores, queries, preferred_element_type=jnp.float32
        )
        return ((acc_keys, acc_values), grad_query.astype(jnp.bfloat16))

    count = queries.shape[0] // block
    zeros = jnp.zeros(keys_all.shape, jnp.float32)
    (acc_keys, acc_values), grad_query = lax.scan(
        one_block, (zeros, zeros), lax.iota(jnp.int32, count)
    )
    return (
        grad_query.reshape(queries.shape),
        acc_keys.astype(jnp.bfloat16),
        acc_values.astype(jnp.bfloat16),
    )


def per_device(
    hidden_in,
    memory,
    segment_ids,
    image_ids,
    attn_in,
    attn_out,
    mlp_in,
    mlp_out,
    gains,
    shifts,
    mlp_bias,
    cotangent,
):
    gathered = (
        lax.all_gather(attn_in, "narrow", axis=1, tiled=True),
        lax.all_gather(attn_out, "narrow", axis=1, tiled=True),
        lax.all_gather(mlp_in, "narrow", axis=0, tiled=True),
        lax.all_gather(mlp_out, "narrow", axis=0, tiled=True),
        lax.all_gather(gains, "narrow", axis=1, tiled=True),
        lax.all_gather(shifts, "narrow", axis=1, tiled=True),
        lax.all_gather(mlp_bias, "narrow", axis=0, tiled=True),
    )
    w_in, w_out, w_up, w_down = (gathered[0], gathered[1], gathered[2], gathered[3])
    gain_all = gathered[4].astype(jnp.float32)
    shift_all = gathered[5].astype(jnp.float32)
    up_bias = gathered[6].astype(jnp.float32)
    tokens = hidden_in[0].astype(jnp.float32)
    rows, width = tokens.shape
    heads = HEADS
    scale = (width // heads) ** (-0.5)
    block = min(512, rows)
    segments = segment_ids[0]
    seg_count = image_ids.shape[1]
    token_image = jnp.sum(
        jnp.where(
            segments[:, None] == lax.iota(jnp.int32, seg_count)[None, :], image_ids[0][None, :], 0
        ),
        axis=1,
    )
    mem_flat = memory[0].reshape(-1, width)
    key_image = lax.iota(jnp.int32, mem_flat.shape[0]) // memory.shape[2]
    mask_self = self_mask(segments)
    mask_cross = cross_mask(token_image, key_image)
    normed_one = layer_norm(tokens, gain_all[0], shift_all[6]).astype(jnp.bfloat16)
    self_query = ((matmul(normed_one, w_in[0]) + shift_all[0]) * scale).astype(jnp.bfloat16)
    self_keys = matmul(normed_one, w_in[1]).astype(jnp.bfloat16)
    self_values = (matmul(normed_one, w_in[2]) + shift_all[1]).astype(jnp.bfloat16)
    self_mix, self_total = attention_forward(
        split_heads(self_query, heads),
        split_heads(self_keys, heads),
        split_heads(self_values, heads),
        mask_self,
        block,
    )
    self_mix = self_mix.reshape(rows, width)
    after_self = tokens + matmul(self_mix, w_out[0]) + shift_all[2]
    normed_two = layer_norm(after_self, gain_all[1], shift_all[7]).astype(jnp.bfloat16)
    cross_query = ((matmul(normed_two, w_in[3]) + shift_all[3]) * scale).astype(jnp.bfloat16)
    cross_keys = matmul(mem_flat, w_in[4]).astype(jnp.bfloat16)
    cross_values = (matmul(mem_flat, w_in[5]) + shift_all[4]).astype(jnp.bfloat16)
    cross_mix, cross_total = attention_forward(
        split_heads(cross_query, heads),
        split_heads(cross_keys, heads),
        split_heads(cross_values, heads),
        mask_cross,
        block,
    )
    cross_mix = cross_mix.reshape(rows, width)
    after_cross = after_self + matmul(cross_mix, w_out[1]) + shift_all[5]
    normed_three = layer_norm(after_cross, gain_all[2], shift_all[8]).astype(jnp.bfloat16)
    pre_act = matmul(normed_three, w_up) + up_bias
    activated = gelu_exact(pre_act).astype(jnp.bfloat16)
    result = after_cross + matmul(activated, w_down) + shift_all[9]
    regathered = (
        lax.all_gather(attn_in, "narrow", axis=1, tiled=True),
        lax.all_gather(attn_out, "narrow", axis=1, tiled=True),
        lax.all_gather(mlp_in, "narrow", axis=0, tiled=True),
        lax.all_gather(mlp_out, "narrow", axis=0, tiled=True),
        lax.all_gather(gains, "narrow", axis=1, tiled=True),
        lax.all_gather(shifts, "narrow", axis=1, tiled=True),
        lax.all_gather(mlp_bias, "narrow", axis=0, tiled=True),
    )
    w_in, w_out, w_up, w_down = (regathered[0], regathered[1], regathered[2], regathered[3])
    gain_all = regathered[4].astype(jnp.float32)
    grad_result = cotangent[0].astype(jnp.float32)
    grad_shift9 = jnp.sum(grad_result, axis=0)
    grad_low = grad_result.astype(jnp.bfloat16)
    grad_down = left_grad(activated, grad_low)
    grad_act = right_grad(grad_low, w_down)
    grad_pre = jax.vjp(gelu_exact, pre_act)[1](grad_act)[0].astype(jnp.bfloat16)
    grad_up_bias = jnp.sum(grad_pre.astype(jnp.float32), axis=0)
    grad_up = left_grad(normed_three, grad_pre)
    grad_norm_three = right_grad(grad_pre, w_up)
    norm_pull = jax.vjp(layer_norm, after_cross, gain_all[2], shift_all[8])[1]
    grad_from_norm, grad_gain3, grad_shift8 = norm_pull(grad_norm_three)
    grad_cross_res = grad_result + grad_from_norm
    grad_shift5 = jnp.sum(grad_cross_res, axis=0)
    grad_branch = grad_cross_res.astype(jnp.bfloat16)
    grad_out_cross = left_grad(cross_mix, grad_branch)
    grad_cross_mix = right_grad(grad_branch, w_out[1]).astype(jnp.bfloat16)
    grad_cq, grad_ck, grad_cv = attention_backward(
        split_heads(cross_query, heads),
        split_heads(cross_keys, heads),
        split_heads(cross_values, heads),
        split_heads(grad_cross_mix, heads),
        cross_total,
        mask_cross,
        block,
    )
    grad_cq = (grad_cq.reshape(rows, width).astype(jnp.float32) * scale).astype(jnp.bfloat16)
    grad_ck = grad_ck.reshape(-1, width)
    grad_cv = grad_cv.reshape(-1, width)
    grad_in3 = left_grad(normed_two, grad_cq)
    grad_shift3 = jnp.sum(grad_cq.astype(jnp.float32), axis=0)
    grad_in4 = left_grad(mem_flat, grad_ck)
    grad_in5 = left_grad(mem_flat, grad_cv)
    grad_shift4 = jnp.sum(grad_cv.astype(jnp.float32), axis=0)
    grad_mem_flat = right_grad(grad_ck, w_in[4]) + right_grad(grad_cv, w_in[5])
    grad_norm_two = right_grad(grad_cq, w_in[3])
    norm_pull = jax.vjp(layer_norm, after_self, gain_all[1], shift_all[7])[1]
    grad_from_norm, grad_gain2, grad_shift7 = norm_pull(grad_norm_two)
    grad_self_res = grad_cross_res + grad_from_norm
    grad_shift2 = jnp.sum(grad_self_res, axis=0)
    grad_branch = grad_self_res.astype(jnp.bfloat16)
    grad_out_self = left_grad(self_mix, grad_branch)
    grad_self_mix = right_grad(grad_branch, w_out[0]).astype(jnp.bfloat16)
    grad_sq, grad_sk, grad_sv = attention_backward(
        split_heads(self_query, heads),
        split_heads(self_keys, heads),
        split_heads(self_values, heads),
        split_heads(grad_self_mix, heads),
        self_total,
        mask_self,
        block,
    )
    grad_sq = (grad_sq.reshape(rows, width).astype(jnp.float32) * scale).astype(jnp.bfloat16)
    grad_sk = grad_sk.reshape(rows, width)
    grad_sv = grad_sv.reshape(rows, width)
    grad_in0 = left_grad(normed_one, grad_sq)
    grad_shift0 = jnp.sum(grad_sq.astype(jnp.float32), axis=0)
    grad_in1 = left_grad(normed_one, grad_sk)
    grad_in2 = left_grad(normed_one, grad_sv)
    grad_shift1 = jnp.sum(grad_sv.astype(jnp.float32), axis=0)
    grad_norm_one = (
        right_grad(grad_sq, w_in[0]) + right_grad(grad_sk, w_in[1]) + right_grad(grad_sv, w_in[2])
    )
    norm_pull = jax.vjp(layer_norm, tokens, gain_all[0], shift_all[6])[1]
    grad_from_norm, grad_gain1, grad_shift6 = norm_pull(grad_norm_one)
    grad_tokens = grad_self_res + grad_from_norm
    grad_gains = jnp.stack([grad_gain1, grad_gain2, grad_gain3])
    grad_shifts = jnp.stack(
        [
            grad_shift0,
            grad_shift1,
            grad_shift2,
            grad_shift3,
            grad_shift4,
            grad_shift5,
            grad_shift6,
            grad_shift7,
            grad_shift8,
            grad_shift9,
        ]
    )
    grad_attn_in = jnp.stack([grad_in0, grad_in1, grad_in2, grad_in3, grad_in4, grad_in5])
    grad_attn_out = jnp.stack([grad_out_self, grad_out_cross])
    owned = (
        lax.psum_scatter(grad_attn_in, "narrow", scatter_dimension=1, tiled=True),
        lax.psum_scatter(grad_attn_out, "narrow", scatter_dimension=1, tiled=True),
        lax.psum_scatter(grad_up, "narrow", scatter_dimension=0, tiled=True),
        lax.psum_scatter(grad_down, "narrow", scatter_dimension=0, tiled=True),
        lax.psum_scatter(grad_gains, "narrow", scatter_dimension=1, tiled=True),
        lax.psum_scatter(grad_shifts, "narrow", scatter_dimension=1, tiled=True),
        lax.psum_scatter(grad_up_bias, "narrow", scatter_dimension=0, tiled=True),
    )
    totals = lax.psum(
        (owned[0], owned[1], owned[2], owned[3], owned[4], owned[5], owned[6]), "wide"
    )
    return (
        result.astype(jnp.bfloat16)[None],
        grad_tokens[None],
        grad_mem_flat.reshape(memory.shape),
        totals[0],
        totals[1],
        totals[2],
        totals[3],
        totals[4],
        totals[5],
        totals[6],
    )


def solution(mesh):
    return jax.shard_map(
        per_device,
        mesh=mesh,
        in_specs=(
            P(("wide", "narrow"), None, None),
            P(("wide", "narrow"), None, None, None),
            P(("wide", "narrow"), None),
            P(("wide", "narrow"), None),
            P(None, "narrow", None),
            P(None, "narrow", None),
            P("narrow", None),
            P("narrow", None),
            P(None, "narrow"),
            P(None, "narrow"),
            P("narrow"),
            P(("wide", "narrow"), None, None),
        ),
        out_specs=(
            P(("wide", "narrow"), None, None),
            P(("wide", "narrow"), None, None),
            P(("wide", "narrow"), None, None, None),
            P(None, "narrow", None),
            P(None, "narrow", None),
            P("narrow", None),
            P("narrow", None),
            P(None, "narrow"),
            P(None, "narrow"),
            P("narrow"),
        ),
        check_vma=False,
    )
```

profile of v0, /device:TPU:0, one launch (start us, length us, event | category | flops | bytes accessed | tf_op | source)
XLA Modules:
  0.0 2148.6 jit_solution(1553855187148448845)
XLA Ops:
  10.1 14.8 all_gather.27
  25.5 19.2 all_gather.26
  51.9 14.2 all_gather.31
  67.1 163.7 %all-gather.5.cloned.1.call-done = bf16[6,1024,1024]{2,1,0:T(8,128)(2,1)} async-done(((bf16[6,256,1024]{2,1,0:T(8,128)(2,1)}), bf16[6,1024,1024]{2,1,0:T(8,128)(2,1)}) %all-gather.5.cloned.1.call-update) | async-done | bytes 12582928 | tf_op jit(solution)/shard_map/all_gather | solution.py:129
  230.8 2.9 add_convert_fusion.5
  235.3 2.9 multiply_convert_fusion.6
  239.5 4.1 fusion.56
  245.1 6.8 add_convert_fusion.1
  251.9 4.4 copy.82
  256.3 9.5 select_reduce_fusion.1
  265.8 8.8 fusion.8
  274.7 9.5 fusion.53
  284.2 27.2 %all-gather.7.cloned.1.call-done = bf16[2,1024,1024]{2,1,0:T(8,128)(2,1)} async-done(((bf16[2,256,1024]{2,1,0:T(8,128)(2,1)}), bf16[2,1024,1024]{2,1,0:T(8,128)(2,1)}) %all-gather.7.cloned.1.call-update) | async-done | bytes 4194320 | tf_op jit(solution)/shard_map/all_gather | solution.py:130
  311.4 3.3 fusion.101
  316.0 4.0 multiply_convert_fusion.5
  322.5 5.7 convolution_convert_fusion.1
  328.1 3.0 copy.84
  331.1 16.9 select_reduce_fusion
  348.0 17.0 fusion
  365.0 17.8 fusion.60
  382.8 4.0 fusion.102
  388.5 72.7 %all-gather.9.cloned.1.call-done = bf16[1024,4096]{1,0:T(8,128)(2,1)} async-done(((bf16[256,4096]{1,0:T(8,128)(2,1)}), bf16[1024,4096]{1,0:T(8,128)(2,1)}) %all-gather.9.cloned.1.call-update) | async-done | bytes 8388624 | tf_op jit(solution)/shard_map/all_gather | solution.py:131
  461.2 27.9 %multiply_convert_fusion.2 = (bf16[512,4096]{1,0:T(8,128)(2,1)}, f32[512,4096]{1,0:T(8,128)}, f32[512,4096]{1,0:T(8,128)}) fusion(f32[4096]{0:T(1024)S(1)} %copy-done.60, bf16[1024,4096]{1,0:T(8,128)(2,1)} %all-gather.9.cloned.1.call-done, f32[512,1024]{1,0:T(8,128)} %copy-done.11, f32[1024]{0:T(1024)S(1)} %bitcast.313, f32[1024]{0:T(1024)S(1)} %bitcast.299, ...), kind=kOutput, calls=%fused_computation.28 | convolution fusion | flops 4436000768 | bytes 31485952 | tf_op jit(solution)/shard_map/dot_general | solution.py:24
  489.1 121.4 %all-gather.11.cloned.1.call-done = bf16[4096,1024]{1,0:T(8,128)(2,1)} async-done(((bf16[1024,1024]{1,0:T(8,128)(2,1)}), bf16[4096,1024]{1,0:T(8,128)(2,1)}) %all-gather.11.cloned.1.call-update) | async-done | bytes 8388624 | tf_op jit(solution)/shard_map/all_gather | solution.py:132
  610.5 14.7 convert_reduce_fusion
  627.2 8.0 multiply_reduce_fusion.2
  636.8 3.4 convolution_bitcast_fusion
  644.8 29.6 %multiply_reduce_fusion = (f32[16,512]{1,0:T(8,128)S(1)}, f32[16,512,1176]{1,2,0:T(8,128)}) fusion(f32[16,512,1176]{1,2,0:T(8,128)} %get-tuple-element.205, f32[16,512]{1,0:T(8,128)S(1)} %log_add_fusion.1, pred[512,1176]{0,1:T(8,128)(4,1)S(1)} %broadcast_compare_fusion, bf16[512,16,64]{0,2,1:T(8,128)(2,1)} %bitcast.265, bf16[1176,16,64]{0,2,1:T(8,128)(2,1)S(1)} %bitcast.258), kind=kOutput, calls=%fused_computation.1 | convolution fusion | flops 1271652352 | bytes 81195008 | tf_op jit(solution)/shard_map/while/body/eval_jaxpr/qhe,khe->hqk/dot_general | solution.py:89
  674.4 31.7 %multiply_convert_fusion = bf16[16,512,1176]{1,2,0:T(8,128)(2,1)} fusion(f32[16,512,1176]{1,2,0:T(8,128)} %get-tuple-element.211, f32[16,512,1176]{1,2,0:T(8,128)} %get-tuple-element.205, f32[16,512]{1,0:T(8,128)S(1)} %get-tuple-element.210, f32[16,512]{1,0:T(8,128)S(1)} %log_add_fusion.1, pred[512,1176]{0,1:T(8,128)(4,1)S(1)} %broadcast_compare_fusion), kind=kLoop, calls=%fused_computation | loop fusion | flops 48168960 | bytes 97005568 | tf_op jit(solution)/shard_map/while/body/eval_jaxpr/convert_element_type | solution.py:93
  706.2 10.4 convert_reduce_fusion.4
  716.7 4.0 multiply_reduce_fusion.3
  726.7 4.1 pad_maximum_fusion
  732.4 10.5 fusion.85
  744.0 10.4 fusion.63
  756.1 3.9 fusion.55
  761.7 12.0 multiply_reduce_fusion.1
  773.7 12.4 multiply_convert_fusion.1
  788.6 3.5 bitcast_dynamic-update-slice_fusion.5
  792.1 2.6 convolution_convert_fusion.2
  795.7 3.6 bitcast_dynamic-update-slice_fusion.4
  799.3 8.7 convert_reduce_fusion.5
  808.0 3.5 bitcast_dynamic-update-slice_fusion.3
  811.5 3.6 bitcast_dynamic-update-slice_fusion.2
  815.1 10.1 convolution_convert_fusion
  825.2 7.2 bitcast_dynamic-update-slice_fusion.1
  832.5 16.2 convert_reduce_fusion.1
  850.1 4.5 bitcast_dynamic-update-slice_fusion
  855.9 3.0 fusion.40
  858.9 3.0 fusion.42
  861.9 3.5 fusion.94
  869.2 4.4 reduce-scatter.11.cloned.1.call-done
  873.6 283.3 %reduce-scatter.13.cloned.1.call-done = f32[256,4096]{1,0:T(8,128)} async-done(((f32[1024,4096]{1,0:T(8,128)}), f32[256,4096]{1,0:T(8,128)}) %reduce-scatter.13.cloned.1.call-update) | async-done | bytes 4194320 | tf_op jit(solution)/shard_map/reduce_scatter | solution.py:284
  1156.9 283.6 %reduce-scatter.15.cloned.1.call-done = f32[1024,1024]{1,0:T(8,128)} async-done(((f32[4096,1024]{1,0:T(8,128)}), f32[1024,1024]{1,0:T(8,128)}) %reduce-scatter.15.cloned.1.call-update) | async-done | bytes 4194320 | tf_op jit(solution)/shard_map/reduce_scatter | solution.py:285
  1440.5 417.5 %reduce-scatter.9.cloned.1.call-done = f32[6,256,1024]{2,1,0:T(8,128)} async-done(((f32[6,1024,1024]{2,1,0:T(8,128)}), f32[6,256,1024]{2,1,0:T(8,128)}) %reduce-scatter.9.cloned.1.call-update) | async-done | bytes 6291472 | tf_op jit(solution)/shard_map/reduce_scatter | solution.py:282
  1859.9 5.5 fusion.50
  1865.4 6.9 convolution_add_fusion
  1872.3 5.1 reshape.479
  1877.4 8.3 copy.92
  1885.7 19.7 all-reduce
  1905.4 3.8 add_bitcast_fusion
  1909.2 9.6 fusion.61
  1919.8 24.8 %all-reduce.1 = (f32[3,256]{1,0:T(4,128)}, f32[10,256]{1,0:T(8,128)}, f32[1024]{0:T(1024)}) all-reduce(f32[3,256]{1,0:T(4,128)S(1)} %copy.100, f32[10,256]{1,0:T(8,128)} %reduce-scatter.17.cloned.1.call-done, f32[1024]{0:T(1024)S(1)} %dynamic-slice.1), channel_id=1, replica_groups=mesh['wide'=8,'narrow'=4] {'wide'}, use_global_device_ids=true, to_apply=%region_31.32 | all-reduce | flops 4352 | bytes 34816 | tf_op jit(solution)/shard_map/psum | solution.py:290
  1944.6 181.8 %all-reduce.5.cloned.1.call-done = (f32[6,256,1024]{2,1,0:T(8,128)}, f32[2,256,1024]{2,1,0:T(8,128)}, f32[256,4096]{1,0:T(8,128)}, f32[1024,1024]{1,0:T(8,128)}) async-done(((f32[6,256,1024]{2,1,0:T(8,128)}, f32[2,256,1024]{2,1,0:T(8,128)}, f32[256,4096]{1,0:T(8,128)}, f32[1024,1024]{1,0:T(8,128)}), (f32[6,256,1024]{2,1,0:T(8,128)}, f32[2,256,1024]{2,1,0:T(8,128)}, f32[256,4096]{1,0:T(8,128)}, ...) | async-done | bytes 16777232 | tf_op jit(solution)/shard_map/psum | solution.py:290
  2126.5 6.8 copy.110
  (257 shorter events, 62.4 us)
Async XLA Ops:
  7.2 18.3 copy-start.77
  7.2 38.1 %copy-start.2 = (bf16[1,512,1024]{2,1,0:T(8,128)(2,1)S(1)}, bf16[1,512,1024]{2,1,0:T(8,128)(2,1)}, u32[]{:S(2)}) copy-start(bf16[1,512,1024]{2,1,0:T(8,128)(2,1)} %param.12) | copy-start | bytes 3145732
  7.2 223.6 %all-gather.5.cloned.1.call-start = ((), (), s32[]{:S(2)}) async-start(), calls=%async_computation.6 | async-start | bytes 15728640 | tf_op jit(solution)/shard_map/all_gather | solution.py:129
  7.9 38.6 %copy-start.51 = (s32[1,512]{1,0:T(1,128)S(1)}, s32[1,512]{1,0:T(1,128)}, u32[]{:S(2)}) copy-start(s32[1,512]{1,0:T(1,128)} %param.14) | copy-start | bytes 6148
  8.0 303.4 %all-gather.7.cloned.1.call-start = ((), (), s32[]{:S(2)}) async-start(), calls=%async_computation.7 | async-start | bytes 5242880 | tf_op jit(solution)/shard_map/all_gather | solution.py:130
  8.7 452.5 %all-gather.9.cloned.1.call-start = ((), (), s32[]{:S(2)}) async-start(), calls=%async_computation.8 | async-start | bytes 10485760 | tf_op jit(solution)/shard_map/all_gather | solution.py:131
  9.4 601.0 %all-gather.11.cloned.1.call-start = ((), (), s32[]{:S(2)}) async-start(), calls=%async_computation.9 | async-start | bytes 10485760 | tf_op jit(solution)/shard_map/all_gather | solution.py:132
  10.0 863.6 %reduce-scatter.11.cloned.1.call-start = ((), (), s32[]{:S(2)}) async-start(), calls=%async_computation.11 | async-start | bytes 10485760 | tf_op jit(solution)/shard_map/reduce_scatter | solution.py:283
  25.5 214.0 %copy-start.71 = (f32[1,1024]{1,0:T(1,128)}, f32[1,1024]{1,0:T(1,128)S(1)}, u32[]{:S(2)}) copy-start(f32[1,1024]{1,0:T(1,128)S(1)} %get-tuple-element.195) | copy-start | bytes 12292
  25.5 289.6 %copy-start.69 = (f32[1,1024]{1,0:T(1,128)}, f32[1,1024]{1,0:T(1,128)S(1)}, u32[]{:S(2)}) copy-start(f32[1,1024]{1,0:T(1,128)S(1)} %get-tuple-element.190) | copy-start | bytes 12292
  45.3 194.2 %copy-start.46 = (f32[1,1024]{1,0:T(1,128)}, f32[1,1024]{1,0:T(1,128)S(1)}, u32[]{:S(2)}) copy-start(f32[1,1024]{1,0:T(1,128)S(1)} %get-tuple-element.199) | copy-start | bytes 12292
  45.3 269.8 %copy-start.62 = (f32[1,1024]{1,0:T(1,128)}, f32[1,1024]{1,0:T(1,128)S(1)}, u32[]{:S(2)}) copy-start(f32[1,1024]{1,0:T(1,128)S(1)} %get-tuple-element.198) | copy-start | bytes 12292
  45.5 194.0 %copy-start.48 = (f32[512]{0:T(512)}, f32[512]{0:T(512)S(1)}, u32[]{:S(2)}) copy-start(f32[512]{0:T(512)S(1)} %broadcast_multiply_fusion.2) | copy-start | bytes 6148
  45.9 193.6 %copy-start.58 = (f32[512]{0:T(512)}, f32[512]{0:T(512)S(1)}, u32[]{:S(2)}) copy-start(f32[512]{0:T(512)S(1)} %fusion.77) | copy-start | bytes 6148
  47.4 4.4 copy-start.79
  47.4 4.5 copy-start.78
  245.1 11.2 copy-start.6
  251.9 4.4 copy-start.21
  265.8 8.8 copy-start.42
  265.8 8.9 copy-start.24
  274.6 9.6 copy-start.44
  314.7 5.4 copy-start.54
  315.0 5.0 copy-start.56
  315.1 5.0 copy-start.65
  316.0 6.5 copy-start.34
  331.1 16.9 copy-start
  348.0 17.0 copy-start.5
  365.0 17.8 copy-start.75
  382.8 78.4 %copy-start.60 = (f32[4096]{0:T(1024)S(1)}, f32[4096]{0:T(1024)}, u32[]{:S(2)}) copy-start(f32[4096]{0:T(1024)} %convert_element_type.231) | copy-start | bytes 49156
  382.8 78.4 %copy-start.64 = (f32[1,1024]{1,0:T(1,128)S(1)}, f32[1,1024]{1,0:T(1,128)}, u32[]{:S(2)}) copy-start(f32[1,1024]{1,0:T(1,128)} %get-tuple-element.197) | copy-start | bytes 12292
  382.8 78.4 %copy-start.74 = (f32[1,1024]{1,0:T(1,128)S(1)}, f32[1,1024]{1,0:T(1,128)}, u32[]{:S(2)}) copy-start(f32[1,1024]{1,0:T(1,128)} %get-tuple-element.188) | copy-start | bytes 12292
  610.5 16.7 copy-start.12
  635.9 4.3 copy-start.9
  674.4 31.7 %copy-start.1 = (bf16[1176,1024]{0,1:T(8,128)(2,1)S(1)}, bf16[1176,1024]{0,1:T(8,128)(2,1)}, u32[]{:S(2)}) copy-start(bf16[1176,1024]{0,1:T(8,128)(2,1)} %copy-done) | copy-start | bytes 7225348
  706.2 10.5 copy-start.18
  706.2 10.5 copy-start.55
  706.2 10.5 copy-start.63
  706.2 10.5 copy-start.66
  716.6 4.0 copy-start.37
  716.7 4.0 copy-start.57
  730.8 426.1 %reduce-scatter.13.cloned.1.call-start = ((), (), s32[]{:S(2)}) async-start(), calls=%async_computation.12 | async-start | bytes 20971520 | tf_op jit(solution)/shard_map/reduce_scatter | solution.py:284
  742.8 697.6 %reduce-scatter.15.cloned.1.call-start = ((), (), s32[]{:S(2)}) async-start(), calls=%async_computation.13 | async-start | bytes 20971520 | tf_op jit(solution)/shard_map/reduce_scatter | solution.py:285
  754.5 7.2 copy-start.43
  754.5 7.2 copy-start.45
  754.5 7.2 copy-start.22
  754.5 1103.5 %reduce-scatter.9.cloned.1.call-start = ((), (), s32[]{:S(2)}) async-start(), calls=%async_computation.10 | async-start | bytes 31457280 | tf_op jit(solution)/shard_map/reduce_scatter | solution.py:282
  761.6 12.1 copy-start.25
  773.7 12.4 copy-start.7
  811.5 3.6 copy-start.4
  825.2 7.2 copy-start.20
  825.2 7.2 copy-start.23
  832.4 17.7 copy-start.35
  854.7 4.2 copy-start.33
  854.7 1064.2 %reduce-scatter.19.cloned.1.call-start = ((), (), s32[]{:S(2)}) async-start(), calls=%async_computation.15 | async-start | bytes 655360
  861.9 4.5 copy-start.73
  867.4 1052.4 %reduce-scatter.17.cloned.1.call-start = ((), (), s32[]{:S(2)}) async-start(), calls=%async_computation.14 | async-start | bytes 81920 | tf_op jit(solution)/shard_map/reduce_scatter | solution.py:287
  869.1 1257.3 %all-reduce.5.cloned.1.call-start = ((), (), s32[]{:S(2)}) async-start(), calls=%async_computation.16 | async-start | bytes 33554432 | tf_op jit(solution)/shard_map/psum | solution.py:290
  1859.8 5.5 copy-start.82
  1877.4 8.3 copy-start.61
  1885.7 23.5 %copy-start.68 = (f32[1,1024]{1,0:T(1,128)S(1)}, f32[1,1024]{1,0:T(1,128)}, u32[]{:S(2)}) copy-start(f32[1,1024]{1,0:T(1,128)} %get-tuple-element.187) | copy-start | bytes 12292
  1905.4 3.8 copy-start.14
  1905.4 3.8 copy-start.88
  2126.5 6.8 copy-start.36
  2136.2 3.7 copy-start.27
  (37 other events, 81.9 us)
Sparse Core Ops, SparseCore 0:
  9.6 221.1 all-gather.4
  232.4 78.9 all-gather.6
  313.0 148.1 all-gather.8
  462.6 147.8 all-gather.10
  730.9 142.6 reduce-scatter.10
  875.8 281.0 reduce-scatter.12
  1159.4 281.0 reduce-scatter.14
  1442.8 415.0 reduce-scatter.8
  1860.9 23.4 reduce-scatter.18
  1886.5 17.3 reduce-scatter.16
  1908.2 218.1 all-reduce.4
where the time goes:
time: 2150 us
  waiting for transfers between devices  1560 us (73%)
  matrix products  322 us (15%)
  blocking collectives  92.6 us (4%)
  other arithmetic  84.2 us (4%)
  local copies, waits for them, and re-layouts  75.2 us (3%)
    reduce_scatter x1, waiting for transfers between devices, per_device(): lax.psum_scatter(grad_attn_in, 'narrow', scatter_dimension=1, tiled=True)  417 us
    reduce_scatter x1, waiting for transfers between devices, per_device(): lax.psum_scatter(grad_down, 'narrow', scatter_dimension=0, tiled=True)  284 us
    reduce_scatter x1, waiting for transfers between devices, per_device(): lax.psum_scatter(grad_up, 'narrow', scatter_dimension=0, tiled=True)  283 us
    psum x1, waiting for transfers between devices, per_device(): lax.psum((owned[0], owned[1], owned[2], owned[3], owned[4], owned[5], own...  182 us
    all_gather x1, waiting for transfers between devices, per_device(): lax.all_gather(attn_in, 'narrow', axis=1, tiled=True)  164 us
    all_gather x1, waiting for transfers between devices, per_device(): lax.all_gather(mlp_out, 'narrow', axis=0, tiled=True)  121 us
    all_gather x1, waiting for transfers between devices, per_device(): lax.all_gather(mlp_in, 'narrow', axis=0, tiled=True)  72.7 us
    dot_general x10, matrix products, matmul(): return jnp.dot(left, right, preferred_element_type=jnp.float32)  71.3 us
  transfers between devices with their start and end apart: 11, of which 9 were waited for; matrix products, arithmetic and copies ran while one was open for 16% of the time, Pallas kernels for 0%

commit v1 on v0

--- a/solution.py
+++ b/solution.py
@@ -1,7 +1,448 @@
+import functools
+
 import jax
 import jax.numpy as jnp
 from jax import lax
+from jax.experimental import pallas as pl
+from jax.experimental.pallas import tpu as pltpu
 from jax.sharding import PartitionSpec as P
+
+MESH = pl.DeviceIdType.MESH
+F32 = jnp.float32
+BF16 = jnp.bfloat16
+MIB = 1 << 20
+
+
+class Geometry:
+    def __init__(self, mesh, width):
+        self.wide = mesh.shape["wide"]
+        self.narrow = mesh.shape["narrow"]
+        self.a_count = self.wide // 4
+        self.width = width
+        self.rows = width // self.narrow
+        self.core_rows = self.rows // 2
+        self.piece_rows = self.core_rows // self.a_count
+        self.half = width // 2
+        self.quarter = width // 4
+
+    def place(self):
+        w = lax.axis_index("wide")
+        n = lax.axis_index("narrow")
+        self.w, self.n = w, n
+        self.a, self.b, self.c = w // 4, lax.rem(w // 2, 2), lax.rem(w, 2)
+        self.core_at = pl.multiple_of(self.c * self.core_rows, self.core_rows)
+        self.b_at = pl.multiple_of(self.b * self.quarter, self.quarter)
+        self.mine = self.piece_at(self.a, self.c)
+        self.other_core = (w + 1 - 2 * self.c, n)
+        self.b_peer = (w + 2 - 4 * self.b, n)
+
+    def piece_at(self, a, c):
+        return pl.multiple_of(c * self.core_rows + a * self.piece_rows, self.piece_rows)
+
+    def a_of(self, step):
+        return lax.rem(self.a + step, self.a_count)
+
+    def a_peer(self, step):
+        return (self.w + 4 * (self.a_of(step) - self.a), self.n)
+
+    def z_of(self, step):
+        return lax.rem(self.n + step, self.narrow)
+
+    def z_peer(self, step):
+        return (self.w, self.z_of(step))
+
+    def greet(self):
+        barrier = pltpu.get_barrier_semaphore()
+        peers = [self.other_core, self.b_peer]
+        peers += [self.a_peer(i) for i in range(1, self.a_count)]
+        peers += [self.z_peer(i) for i in range(1, self.narrow)]
+        for peer in peers:
+            pl.semaphore_signal(barrier, inc=1, device_id=peer, device_id_type=MESH)
+        pl.semaphore_wait(barrier, len(peers))
+
+
+def remote(src, dst, send, recv, peer):
+    return pltpu.make_async_remote_copy(
+        src_ref=src, dst_ref=dst, send_sem=send, recv_sem=recv, device_id=peer, device_id_type=MESH
+    )
+
+
+class Gather:
+    def __init__(self, geo, own, ring, send, recv):
+        self.geo, self.own, self.ring, self.send, self.recv = geo, own, ring, send, recv
+        self.open = []
+
+    @staticmethod
+    def sems(geo):
+        return 2 * (geo.narrow - 1) + 2 * geo.a_count + 1
+
+    def copy(self, u, slot, src, dst, peer):
+        return remote(src, dst, self.send.at[u, slot], self.recv.at[u, slot], peer)
+
+    def z_copies(self, u):
+        g = self.geo
+        rows = pl.ds(g.mine, g.piece_rows)
+        out = []
+        for k in range(1, g.narrow):
+            for h in range(2):
+                cols = pl.ds(pl.multiple_of(h * g.half + g.b_at, g.quarter), g.quarter)
+                out.append(
+                    self.copy(
+                        u,
+                        2 * (k - 1) + h,
+                        self.own.at[u, rows, cols],
+                        self.ring.at[u, g.narrow - k - 1, rows, cols],
+                        g.z_peer(k),
+                    )
+                )
+        return out
+
+    def p1_copies(self, u):
+        g = self.geo
+        base = 2 * (g.narrow - 1)
+        rows = pl.ds(g.mine, g.piece_rows)
+        low = self.ring.at[u, :, rows, pl.ds(g.b_at, g.quarter)]
+        high = self.ring.at[u, :, rows, pl.ds(pl.multiple_of(g.half + g.b_at, g.quarter), g.quarter)]
+        out = [self.copy(u, base + i - 1, low, low, g.a_peer(i)) for i in range(1, g.a_count)]
+        return out + [self.copy(u, base + g.a_count - 1, high, high, g.b_peer)]
+
+    def p2_copies(self, u):
+        g = self.geo
+        base = 2 * (g.narrow - 1) + g.a_count
+        low = self.ring.at[u, :, pl.ds(g.core_at, g.core_rows), pl.ds(g.b_at, g.quarter)]
+        high = self.ring.at[u, :, pl.ds(g.mine, g.piece_rows), pl.ds(g.half, g.half)]
+        out = [self.copy(u, base + i - 1, high, high, g.a_peer(i)) for i in range(1, g.a_count)]
+        return out + [self.copy(u, base + g.a_count - 1, low, low, g.b_peer)]
+
+    def c_copies(self, u):
+        g = self.geo
+        base = 2 * (g.narrow - 1) + 2 * g.a_count
+        part = self.ring.at[u, :, pl.ds(g.core_at, g.core_rows), :]
+        return [self.copy(u, base, part, part, g.other_core)]
+
+    def begin(self, copies):
+        for copy in copies:
+            copy.start()
+            self.open.append(copy)
+
+    def event(self, kind, u):
+        if kind == 0:
+            self.begin(self.z_copies(u))
+        elif kind == 1:
+            for copy in self.z_copies(u):
+                copy.wait_recv()
+            self.begin(self.p1_copies(u))
+        elif kind == 2:
+            for copy in self.p1_copies(u):
+                copy.wait_recv()
+            self.begin(self.p2_copies(u))
+        elif kind == 3:
+            for copy in self.p2_copies(u):
+                copy.wait_recv()
+            self.begin(self.c_copies(u))
+        else:
+            for copy in self.c_copies(u):
+                copy.wait_recv()
+
+    def finish(self):
+        for copy in self.open:
+            copy.wait_send()
+
+
+def add_rows(dst, parts, tile):
+    count, rows = dst.shape[0], dst.shape[1]
+    tile = min(tile, rows)
+    per = rows // tile
+
+    def body(i, carry):
+        k, r = i // per, pl.multiple_of(lax.rem(i, per) * tile, tile)
+        total = parts[0](k, r, tile).astype(F32)
+        for part in parts[1:]:
+            total = total + part(k, r, tile).astype(F32)
+        dst[k, pl.ds(r, tile), :] = total.astype(dst.dtype)
+        return carry
+
+    lax.fori_loop(0, count * per, body, 0)
+
+
+class Reduce:
+    slots = 3
+    gslots = 3
+
+    def __init__(self, geo, bufs):
+        self.geo = geo
+        (
+            self.gbuf, self.rc, self.s1, self.p1a, self.p1b, self.s2a, self.s2b, self.p2a, self.p2b,
+            self.s3, self.zr, self.out, self.send, self.recv, self.credit,
+        ) = bufs
+        self.order = {}
+        self.open = {}
+        self.units = self.out.shape[0]
+
+    @classmethod
+    def scratch(cls, geo, units):
+        g, n, w = geo, geo.narrow, geo.width
+        peers = max(g.a_count - 1, 1)
+        count = 1 + 4 * g.a_count + (n - 1) + 1
+        return [
+            pltpu.VMEM((cls.gslots, n, g.rows, w), BF16),
+            pltpu.VMEM((cls.slots, n, g.core_rows, w), BF16),
+            pltpu.VMEM((cls.slots, n, g.core_rows, w), BF16),
+            pltpu.VMEM((units, peers, n, g.piece_rows, g.half), BF16),
+            pltpu.VMEM((units, n, g.core_rows, g.quarter), BF16),
+            pltpu.VMEM((cls.slots, n, g.piece_rows, g.half), BF16),
+            pltpu.VMEM((cls.slots, n, g.core_rows, g.quarter), BF16),
+            pltpu.VMEM((units, n, g.piece_rows, g.quarter), BF16),
+            pltpu.VMEM((units, peers, n, g.piece_rows, g.quarter), BF16),
+            pltpu.VMEM((cls.slots, n, g.piece_rows, g.half), BF16),
+            pltpu.VMEM((units, n - 1, g.piece_rows, g.half), BF16),
+        ], [
+            pltpu.SemaphoreType.DMA((units, count)),
+            pltpu.SemaphoreType.DMA((units, count)),
+            pltpu.SemaphoreType.REGULAR,
+        ]
+
+    def copy(self, u, slot, src, dst, peer):
+        return remote(src, dst, self.send.at[u, slot], self.recv.at[u, slot], peer)
+
+    def copies(self, kind, u):
+        g = self.geo
+        q = self.order[u]
+        slot, gslot = q % self.slots, q % self.gslots
+        na = g.a_count
+        steps = range(1, na)
+        low_b = pl.ds(g.b_at, g.quarter)
+        peer_b = pl.multiple_of((1 - g.b) * g.quarter, g.quarter)
+        mine = pl.ds(g.mine, g.piece_rows)
+        core = pl.ds(g.core_at, g.core_rows)
+
+        def in_core(a):
+            return pl.ds(pl.multiple_of(a * g.piece_rows, g.piece_rows), g.piece_rows)
+
+        if kind == 0:
+            other = pl.ds(pl.multiple_of((1 - g.c) * g.core_rows, g.core_rows), g.core_rows)
+            return [self.copy(u, 0, self.gbuf.at[gslot, :, other, :], self.rc.at[slot], g.other_core)]
+        if kind == 1:
+            out = [
+                self.copy(
+                    u, i, self.s1.at[slot, :, in_core(g.a_of(i)), pl.ds(0, g.half)],
+                    self.p1a.at[u, na - i - 1], g.a_peer(i),
+                )
+                for i in steps
+            ]
+            cols = pl.ds(pl.multiple_of(g.half + peer_b, g.quarter), g.quarter)
+            return out + [self.copy(u, na, self.s1.at[slot, :, :, cols], self.p1b.at[u], g.b_peer)]
+        if kind == 2:
+            out = [
+                self.copy(
+                    u, na + i, self.s2b.at[slot, :, in_core(g.a_of(i)), :],
+                    self.p2b.at[u, na - i - 1], g.a_peer(i),
+                )
+                for i in steps
+            ]
+            cols = pl.ds(peer_b, g.quarter)
+            return out + [self.copy(u, 2 * na, self.s2a.at[slot, :, :, cols], self.p2a.at[u], g.b_peer)]
+        if kind == 3:
+            return [
+                self.copy(
+                    u, 2 * na + k, self.s3.at[slot, g.z_of(k)], self.zr.at[u, g.narrow - k - 1], g.z_peer(k)
+                )
+                for k in range(1, g.narrow)
+            ]
+        base = 2 * na + g.narrow
+        if kind == 4:
+            low = self.out.at[u, mine, low_b]
+            high = self.out.at[u, mine, pl.ds(pl.multiple_of(g.half + g.b_at, g.quarter), g.quarter)]
+            out = [self.copy(u, base + i - 1, low, low, g.a_peer(i)) for i in steps]
+            return out + [self.copy(u, base + na - 1, high, high, g.b_peer)]
+        base += na
+        if kind == 5:
+            low = self.out.at[u, core, low_b]
+            high = self.out.at[u, mine, pl.ds(g.half, g.half)]
+            out = [self.copy(u, base + i - 1, high, high, g.a_peer(i)) for i in steps]
+            return out + [self.copy(u, base + na - 1, low, low, g.b_peer)]
+        base += na
+        part = self.out.at[u, core, :]
+        return [self.copy(u, base, part, part, g.other_core)]
+
+    def begin(self, kind, u):
+        copies = self.copies(kind, u)
+        for copy in copies:
+            copy.start()
+        self.open[kind, u] = copies
+
+    def arrived(self, kind, u):
+        for copy in self.copies(kind, u):
+            copy.wait_recv()
+
+    def sent(self, kind, q):
+        for (k, u), copies in list(self.open.items()):
+            if k == kind and self.order[u] == q:
+                for copy in copies:
+                    copy.wait_send()
+                del self.open[k, u]
+
+    def slot_for(self, u):
+        q = len(self.order)
+        self.order[u] = q
+        self.sent(0, q - self.gslots)
+        return q % self.gslots
+
+    def event(self, kind, u):
+        g = self.geo
+        q = self.order[u]
+        slot, gslot = q % self.slots, q % self.gslots
+        na = g.a_count
+        if kind == 0:
+            if q >= self.slots:
+                pl.semaphore_wait(self.credit, 1)
+            self.begin(0, u)
+            return
+        self.arrived(kind - 1, u)
+        self.sent(kind, q - self.slots)
+        if kind == 1:
+            add_rows(
+                self.s1.at[slot],
+                [
+                    lambda k, r, t: self.gbuf[gslot, k, pl.ds(pl.multiple_of(g.core_at + r, 16), t), :],
+                    lambda k, r, t: self.rc[slot, k, pl.ds(r, t), :],
+                ],
+                32,
+            )
+            if q + self.slots < self.units:
+                pl.semaphore_signal(self.credit, inc=1, device_id=g.other_core, device_id_type=MESH)
+        elif kind == 2:
+            own = g.a * g.piece_rows
+            add_rows(
+                self.s2a.at[slot],
+                [lambda k, r, t: self.s1[slot, k, pl.ds(pl.multiple_of(own + r, 16), t), pl.ds(0, g.half)]]
+                + [lambda k, r, t, i=i: self.p1a[u, i, k, pl.ds(r, t), :] for i in range(na - 1)],
+                32,
+            )
+            cols = pl.ds(pl.multiple_of(g.half + g.b_at, g.quarter), g.quarter)
+            add_rows(
+                self.s2b.at[slot],
+                [
+                    lambda k, r, t: self.s1[slot, k, pl.ds(r, t), cols],
+                    lambda k, r, t: self.p1b[u, k, pl.ds(r, t), :],
+                ],
+                64,
+            )
+        elif kind == 3:
+            own = g.a * g.piece_rows
+            cols = pl.ds(g.b_at, g.quarter)
+            add_rows(
+                self.s3.at[slot, :, :, pl.ds(0, g.quarter)],
+                [
+                    lambda k, r, t: self.s2a[slot, k, pl.ds(r, t), cols],
+                    lambda k, r, t: self.p2a[u, k, pl.ds(r, t), :],
+                ],
+                64,
+            )
+            add_rows(
+                self.s3.at[slot, :, :, pl.ds(g.quarter, g.quarter)],
+                [lambda k, r, t: self.s2b[slot, k, pl.ds(pl.multiple_of(own + r, 16), t), :]]
+                + [lambda k, r, t, i=i: self.p2b[u, i, k, pl.ds(r, t), :] for i in range(na - 1)],
+                64,
+            )
+        elif kind == 4:
+            total = self.s3[slot, g.n].astype(F32)
+            for k in range(g.narrow - 1):
+                total = total + self.zr[u, k].astype(F32)
+            total = total.astype(BF16)
+            mine = pl.ds(g.mine, g.piece_rows)
+            self.out[u, mine, pl.ds(g.b_at, g.quarter)] = total[:, : g.quarter]
+            cols = pl.ds(pl.multiple_of(g.half + g.b_at, g.quarter), g.quarter)
+            self.out[u, mine, cols] = total[:, g.quarter :]
+        if kind < 7:
+            self.begin(kind, u)
+
+    def finish(self):
+        for copies in self.open.values():
+            for copy in copies:
+                copy.wait_send()
+        self.open = {}
+
+
+def pack_weights(geo, attn_in, attn_out, mlp_in, mlp_out):
+    n, rows, width = geo.narrow, geo.rows, geo.width
+    up = mlp_in.reshape(rows, n, -1, rows).transpose(2, 0, 1, 3).reshape(-1, rows, width)
+    down = mlp_out.reshape(-1, rows, width)
+    return jnp.concatenate([attn_in, attn_out, up, down], axis=0)
+
+
+def unpack_grads(geo, total, attn_in, attn_out):
+    n, rows, width = geo.narrow, geo.rows, geo.width
+    total = total.astype(F32)
+    i, o = attn_in.shape[0], attn_out.shape[0]
+    ups = (total.shape[0] - i - o) // 2
+    up = total[i + o : i + o + ups].reshape(ups, rows, n, rows).transpose(1, 2, 0, 3)
+    return (
+        total[:i], total[i : i + o], up.reshape(rows, -1), total[i + o + ups :].reshape(-1, width),
+    )
+
+
+def gather_weights(geo, own):
+    units, rows, width = own.shape
+    n = geo.narrow
+    count = Gather.sems(geo)
+
+    def kernel(own_ref, ring_ref, send, recv):
+        geo.place()
+        geo.greet()
+        gather = Gather(geo, own_ref, ring_ref, send, recv)
+        gather.event(0, 0)
+        for s in range(units + 4):
+            if s + 1 < units:
+                gather.event(0, s + 1)
+            for kind in range(1, 5):
+                u = s - kind + 1
+                if 0 <= u < units:
+                    gather.event(kind, u)
+        gather.finish()
+
+    return pl.pallas_call(
+        kernel,
+        out_shape=jax.ShapeDtypeStruct((units, n - 1, rows, width), BF16),
+        in_specs=[pl.BlockSpec(memory_space=pltpu.HBM)],
+        out_specs=pl.BlockSpec(memory_space=pltpu.HBM),
+        scratch_shapes=[pltpu.SemaphoreType.DMA((units, count)), pltpu.SemaphoreType.DMA((units, count))],
+        compiler_params=pltpu.CompilerParams(collective_id=0, has_side_effects=True),
+    )(own)
+
+
+def reduce_grads(geo, grads):
+    units, n, rows, width = grads.shape
+    vmem, sems = Reduce.scratch(geo, units)
+
+    def kernel(grads_ref, out_ref, *bufs):
+        load = bufs[-1]
+        geo.place()
+        geo.greet()
+        red = Reduce(geo, list(bufs[: len(vmem)]) + [out_ref] + list(bufs[len(vmem) : -1]))
+        for s in range(units + 7):
+            if s < units:
+                slot = red.slot_for(s)
+                copy = pltpu.make_async_copy(grads_ref.at[s], red.gbuf.at[slot], load)
+                copy.start()
+                copy.wait()
+            for kind in range(8):
+                u = s - kind
+                if 0 <= u < units:
+                    red.event(kind, u)
+        red.finish()
+
+    return pl.pallas_call(
+        kernel,
+        out_shape=jax.ShapeDtypeStruct((units, rows, width), BF16),
+        in_specs=[pl.BlockSpec(memory_space=pltpu.HBM)],
+        out_specs=pl.BlockSpec(memory_space=pltpu.VMEM),
+        scratch_shapes=vmem + sems + [pltpu.SemaphoreType.DMA],
+        compiler_params=pltpu.CompilerParams(
+            collective_id=1, has_side_effects=True, vmem_limit_bytes=58 * MIB
+        ),
+    )(grads)
+
 
 HEADS = 16
 
@@ -112,6 +553,7 @@
 
 
 def per_device(
+    mesh,
     hidden_in,
     memory,
     segment_ids,
@@ -125,19 +567,21 @@
     mlp_bias,
     cotangent,
 ):
-    gathered = (
-        lax.all_gather(attn_in, "narrow", axis=1, tiled=True),
-        lax.all_gather(attn_out, "narrow", axis=1, tiled=True),
-        lax.all_gather(mlp_in, "narrow", axis=0, tiled=True),
-        lax.all_gather(mlp_out, "narrow", axis=0, tiled=True),
-        lax.all_gather(gains, "narrow", axis=1, tiled=True),
-        lax.all_gather(shifts, "narrow", axis=1, tiled=True),
-        lax.all_gather(mlp_bias, "narrow", axis=0, tiled=True),
-    )
-    w_in, w_out, w_up, w_down = (gathered[0], gathered[1], gathered[2], gathered[3])
-    gain_all = gathered[4].astype(jnp.float32)
-    shift_all = gathered[5].astype(jnp.float32)
-    up_bias = gathered[6].astype(jnp.float32)
+    geo = Geometry(mesh, hidden_in.shape[2])
+    own = pack_weights(geo, attn_in, attn_out, mlp_in, mlp_out)
+    ring = gather_weights(geo, own)
+    place = lax.axis_index("narrow")
+    full = jnp.concatenate([own[:, None], ring], axis=1)
+    full = jnp.take(full, lax.rem(jnp.arange(geo.narrow) - place + geo.narrow, geo.narrow), axis=1)
+    full = full.reshape(full.shape[0], geo.width, geo.width)
+    n_in, n_out = attn_in.shape[0], attn_out.shape[0]
+    n_up = (full.shape[0] - n_in - n_out) // 2
+    w_in, w_out = full[:n_in], full[n_in : n_in + n_out]
+    w_up = full[n_in + n_out : n_in + n_out + n_up].transpose(1, 0, 2).reshape(geo.width, -1)
+    w_down = full[n_in + n_out + n_up :].reshape(-1, geo.width)
+    gain_all = lax.all_gather(gains, "narrow", axis=1, tiled=True).astype(jnp.float32)
+    shift_all = lax.all_gather(shifts, "narrow", axis=1, tiled=True).astype(jnp.float32)
+    up_bias = lax.all_gather(mlp_bias.reshape(n_up, -1), "narrow", axis=1, tiled=True).reshape(-1).astype(jnp.float32)
     tokens = hidden_in[0].astype(jnp.float32)
     rows, width = tokens.shape
     heads = HEADS
@@ -185,17 +629,6 @@
     pre_act = matmul(normed_three, w_up) + up_bias
     activated = gelu_exact(pre_act).astype(jnp.bfloat16)
     result = after_cross + matmul(activated, w_down) + shift_all[9]
-    regathered = (
-        lax.all_gather(attn_in, "narrow", axis=1, tiled=True),
-        lax.all_gather(attn_out, "narrow", axis=1, tiled=True),
-        lax.all_gather(mlp_in, "narrow", axis=0, tiled=True),
-        lax.all_gather(mlp_out, "narrow", axis=0, tiled=True),
-        lax.all_gather(gains, "narrow", axis=1, tiled=True),
-        lax.all_gather(shifts, "narrow", axis=1, tiled=True),
-        lax.all_gather(mlp_bias, "narrow", axis=0, tiled=True),
-    )
-    w_in, w_out, w_up, w_down = (regathered[0], regathered[1], regathered[2], regathered[3])
-    gain_all = regathered[4].astype(jnp.float32)
     grad_result = cotangent[0].astype(jnp.float32)
     grad_shift9 = jnp.sum(grad_result, axis=0)
     grad_low = grad_result.astype(jnp.bfloat16)
@@ -276,20 +709,21 @@
             grad_shift9,
         ]
     )
-    grad_attn_in = jnp.stack([grad_in0, grad_in1, grad_in2, grad_in3, grad_in4, grad_in5])
-    grad_attn_out = jnp.stack([grad_out_self, grad_out_cross])
+    blocks = [grad_in0, grad_in1, grad_in2, grad_in3, grad_in4, grad_in5, grad_out_self, grad_out_cross]
+    width = geo.width
+    blocks += [grad_up[:, j * width : (j + 1) * width] for j in range(n_up)]
+    blocks += [grad_down[j * width : (j + 1) * width] for j in range(n_up)]
+    grads = jnp.stack([g.astype(jnp.bfloat16) for g in blocks])
+    grads = grads.reshape(len(blocks), geo.narrow, geo.rows, width)
+    summed = reduce_grads(geo, grads)
+    bias_parts = grad_up_bias.reshape(n_up, -1)
     owned = (
-        lax.psum_scatter(grad_attn_in, "narrow", scatter_dimension=1, tiled=True),
-        lax.psum_scatter(grad_attn_out, "narrow", scatter_dimension=1, tiled=True),
-        lax.psum_scatter(grad_up, "narrow", scatter_dimension=0, tiled=True),
-        lax.psum_scatter(grad_down, "narrow", scatter_dimension=0, tiled=True),
         lax.psum_scatter(grad_gains, "narrow", scatter_dimension=1, tiled=True),
         lax.psum_scatter(grad_shifts, "narrow", scatter_dimension=1, tiled=True),
-        lax.psum_scatter(grad_up_bias, "narrow", scatter_dimension=0, tiled=True),
-    )
-    totals = lax.psum(
-        (owned[0], owned[1], owned[2], owned[3], owned[4], owned[5], owned[6]), "wide"
-    )
+        lax.psum_scatter(bias_parts, "narrow", scatter_dimension=1, tiled=True),
+    )
+    small = lax.psum(owned, "wide")
+    totals = unpack_grads(geo, summed, attn_in, attn_out) + (small[0], small[1], small[2].reshape(-1))
     return (
         result.astype(jnp.bfloat16)[None],
         grad_tokens[None],
@@ -306,7 +740,7 @@
 
 def solution(mesh):
     return jax.shard_map(
-        per_device,
+        functools.partial(per_device, mesh),
         mesh=mesh,
         in_specs=(
             P(("wide", "narrow"), None, None),

time: 2150 us -> 1070 us (0.50)
  waiting for transfers between devices: 1560 us -> 0.06 us
  Pallas kernels: 0 us -> 315 us
  local copies, waits for them, and re-layouts: 75.2 us -> 237 us
  other arithmetic: 84.2 us -> 133 us
  matrix products: 322 us -> 292 us
  blocking collectives: 92.6 us -> 64.4 us
    reduce_scatter x4 -> x0, waiting for transfers between devices: 989 us -> none  [the longest x1 417 us: per_device(): lax.psum_scatter(grad_attn_in, 'narrow', scatter_dimension=1, tiled=True)]
    all_gather x4 -> x0, waiting for transfers between devices: 385 us -> none  [the longest x1 164 us: per_device(): lax.all_gather(attn_in, 'narrow', axis=1, tiled=True)]
    pallas_call x0 -> x2, Pallas kernels: none -> 315 us  [the longest x1 191 us: reduce_grads(): pl.pallas_call(kernel, out_shape=jax.ShapeDtypeStruct((units, rows, width...]
    psum x1 -> x0, waiting for transfers between devices: 182 us -> none  [per_device(): lax.psum((owned[0], owned[1], owned[2], owned[3], owned[4], owned[5], own...]
    gather x0 -> x32, local copies, waits for them, and re-layouts: none -> 69.2 us
    slice x0 -> x7, local copies, waits for them, and re-layouts: none -> 38.8 us  [the longest x1 13.5 us: per_device(): w_down = full[n_in + n_out + n_up:].reshape(-1, geo.width)]
    concatenate x0 -> x1, other arithmetic: none -> 23.3 us  [per_device(): full = jnp.concatenate([own[:, None], ring], axis=1)]
    select_n x0 -> x2, other arithmetic: none -> 22.8 us  [per_device(): jnp.take(full, lax.rem(jnp.arange(geo.narrow) - place + geo.narrow, geo.n...]
  transfers between devices with their start and end apart: 11 -> 3, of which waited for: 9 -> 0; matrix products, arithmetic and copies ran while one was open for 16% -> 16% of each run, Pallas kernels for 0% -> 18%
where the time goes in v1:
time: 1070 us; the launch traced here: 1060 us
  Pallas kernels  315 us (29%)
  matrix products  292 us (27%)
  local copies, waits for them, and re-layouts  237 us (22%)
  other arithmetic  133 us (12%)
  blocking collectives  64.4 us (6%)
  between operations  15.3 us (1%)
    pallas_call x1, Pallas kernels, reduce_grads(): pl.pallas_call(kernel, out_shape=jax.ShapeDtypeStruct((units, rows, width...  191 us
    pallas_call x1, Pallas kernels, gather_weights(): pl.pallas_call(kernel, out_shape=jax.ShapeDtypeStruct((units, n - 1, rows...  125 us
    dot_general x10, matrix products, matmul(): return jnp.dot(left, right, preferred_element_type=jnp.float32)  69.4 us
    gather x32, local copies, waits for them, and re-layouts  69.2 us
    unnamed x255, local copies, waits for them, and re-layouts  62.7 us
    convert_element_type x2, other arithmetic, one_block(): grad_scores = (probs * (grad_probs - inner)).astype(jnp.bfloat16)  44.1 us
    dot_general x2, matrix products, one_block(): jnp.einsum('qhe,khe->hqk', grad_mixed, values_all, preferred_element_type...  41.7 us
    dot_general x10, matrix products, left_grad(): jnp.einsum('ra,rb->ab', left, right, preferred_element_type=jnp.float32)  39.6 us
  transfers between devices with their start and end apart: 3, of which 0 were waited for; matrix products, arithmetic and copies ran while one was open for 16% of the time, Pallas kernels for 18%

profile of v1, /device:TPU:0, one launch (start us, length us, event | category | flops | bytes accessed | tf_op | source)
XLA Modules:
  0.0 1057.8 jit_solution(3788654163501801277)
XLA Ops:
  16.6 8.2 fusion.90
  24.8 124.7 %shard_map.195 = bf16[16,3,256,1024]{3,2,1,0:T(8,128)(2,1)} custom-call(bf16[16,256,1024]{2,1,0:T(8,128)(2,1)} %get-tuple-element.270.own_ref), custom_call_target="tpu_custom_call" | custom-call | tf_op jit(solution)/shard_map/pallas_call | solution.py:404
  149.5 23.3 %fusion.14 = (bf16[16,4,256,256]{3,2,1,0:T(8,128)(2,1)}, bf16[16,4,256,256]{3,2,1,0:T(8,128)(2,1)}, bf16[16,4,256,256]{3,2,1,0:T(8,128)(2,1)}, bf16[16,4,256,256]{3,2,1,0:T(8,128)(2,1)}) fusion(bf16[16,3,256,1024]{3,2,1,0:T(8,128)(2,1)} %shard_map.195, bf16[16,1,256,1024]{3,2,1,0:T(8,128)(2,1)} %get-tuple-element.269), kind=kLoop, calls=%fused_computation.40 | loop fusion | flops 67108864 | bytes 67108864 | tf_op jit(solution)/shard_map/concatenate | solution.py:574
  172.7 4.2 broadcast.488.clone2
  177.0 17.3 %while.7 = (s32[]{:T(128)}, bf16[16,4,256,256]{3,2,1,0:T(8,128)(2,1)}, s32[4,1]{0,1:T(1,128)S(1)}, bf16[4,16,256,256]{3,2,0,1:T(8,128)(2,1)}, s32[]{:T(128)}) while((s32[]{:T(128)}, bf16[16,4,256,256]{3,2,1,0:T(8,128)(2,1)}, s32[4,1]{0,1:T(1,128)S(1)}, bf16[4,16,256,256]{3,2,0,1:T(8,128)(2,1)}, s32[]{:T(128)}) %tuple.123), condition=%wide.while_cond.3, body=%wide.while_body.3.sunk | while | flops 2 | bytes 4194901 | solution.py:575
  177.5 3.8 bitcast_dynamic-update-slice_fusion.11
  186.2 3.8 bitcast_dynamic-update-slice_fusion.11
  190.5 3.8 bitcast_dynamic-update-slice_fusion.11
  194.3 4.3 broadcast.488.clone2.1
  198.5 17.3 %while.6 = (s32[]{:T(128)}, bf16[16,4,256,256]{3,2,1,0:T(8,128)(2,1)}, s32[4,1]{0,1:T(1,128)S(1)}, bf16[4,16,256,256]{3,2,0,1:T(8,128)(2,1)}, s32[]{:T(128)}) while((s32[]{:T(128)}, bf16[16,4,256,256]{3,2,1,0:T(8,128)(2,1)}, s32[4,1]{0,1:T(1,128)S(1)}, bf16[4,16,256,256]{3,2,0,1:T(8,128)(2,1)}, s32[]{:T(128)}) %tuple.141), condition=%wide.while_cond.2, body=%wide.while_body.2.sunk | while | flops 2 | bytes 4194901 | solution.py:575
  199.1 3.7 bitcast_dynamic-update-slice_fusion.10
  203.4 3.8 bitcast_dynamic-update-slice_fusion.10
  215.8 4.3 broadcast.488.clone2.2
  220.1 17.3 %while.5 = (s32[]{:T(128)}, bf16[16,4,256,256]{3,2,1,0:T(8,128)(2,1)}, s32[4,1]{0,1:T(1,128)S(1)}, bf16[4,16,256,256]{3,2,0,1:T(8,128)(2,1)}, s32[]{:T(128)}) while((s32[]{:T(128)}, bf16[16,4,256,256]{3,2,1,0:T(8,128)(2,1)}, s32[4,1]{0,1:T(1,128)S(1)}, bf16[4,16,256,256]{3,2,0,1:T(8,128)(2,1)}, s32[]{:T(128)}) %tuple.142), condition=%wide.while_cond.1, body=%wide.while_body.1.sunk | while | flops 2 | bytes 4194901 | solution.py:575
  220.6 3.8 bitcast_dynamic-update-slice_fusion.9
  229.3 3.8 bitcast_dynamic-update-slice_fusion.9
  233.6 3.8 bitcast_dynamic-update-slice_fusion.9
  237.4 4.3 broadcast.488.clone2.3
  241.7 17.3 %while.4 = (s32[]{:T(128)}, bf16[16,4,256,256]{3,2,1,0:T(8,128)(2,1)}, s32[4,1]{0,1:T(1,128)S(1)}, bf16[4,16,256,256]{3,2,0,1:T(8,128)(2,1)}, s32[]{:T(128)}) while((s32[]{:T(128)}, bf16[16,4,256,256]{3,2,1,0:T(8,128)(2,1)}, s32[4,1]{0,1:T(1,128)S(1)}, bf16[4,16,256,256]{3,2,0,1:T(8,128)(2,1)}, s32[]{:T(128)}) %tuple.143), condition=%wide.while_cond, body=%wide.while_body.sunk | while | flops 2 | bytes 4194901 | solution.py:575
  242.2 3.7 bitcast_dynamic-update-slice_fusion.8
  246.6 3.8 bitcast_dynamic-update-slice_fusion.8
  258.9 22.8 %maximum_select_fusion = bf16[16,4,256,1024]{3,2,1,0:T(8,128)(2,1)} fusion(bf16[16,4,256,256]{3,2,1,0:T(8,128)(2,1)} %bitcast.308, bf16[16,4,256,256]{3,2,1,0:T(8,128)(2,1)} %bitcast.309, bf16[16,4,256,256]{3,2,1,0:T(8,128)(2,1)} %bitcast.310, bf16[16,4,256,256]{3,2,1,0:T(8,128)(2,1)} %bitcast.307, pred[4]{0:T(512)(128)(4,1)S(1)} %compare_and_fusion), kind=kLoop, calls=%fused_computation.20 | loop fusion | flops 150994944 | bytes 67108864 | tf_op jit(solution)/shard_map/jit(_take)/select_n | solution.py:575
  281.7 10.9 %fusion.97 = (bf16[1,4,256,1024]{3,2,1,0:T(8,128)(2,1)}, bf16[1,4,256,1024]{3,2,1,0:T(8,128)(2,1)}, bf16[1,4,256,1024]{3,2,1,0:T(8,128)(2,1)}, bf16[1,4,256,1024...) fusion(bf16[16,4,256,1024]{3,2,1,0:T(8,128)(2,1)} %maximum_sele, ...), kind=kLoop, calls=%fused_computation.223 | loop fusion | bytes 33554432 | tf_op jit(solution)/shard_map/slice | solution.py:627
  292.7 13.5 %fusion.96 = (bf16[4,4,256,1024]{3,2,1,0:T(8,128)(2,1)}, bf16[4,4,256,1024]{3,2,1,0:T(8,128)(2,1)}) fusion(bf16[16,4,256,1024]{3,2,1,0:T(8,128)(2,1)} %maximum_select_fusion), kind=kLoop, calls=%fused_computation.222 | loop fusion | bytes 33554432 | tf_op jit(solution)/shard_map/slice | solution.py:581
  306.2 16.2 %all_gather.10 = bf16[10,1024]{1,0:T(8,128)(2,1)S(1)} all-gather(bf16[10,256]{1,0:T(8,128)(2,1)S(1)} %copy-done.95), channel_id=1, replica_groups=mesh['wide'=8,'narrow'=4] {'narrow'}, dimensions={1}, use_global_device_ids=true | all-gather | bytes 25600 | tf_op jit(solution)/shard_map/all_gather | solution.py:583
  322.9 12.1 %all_gather.9 = bf16[3,1024]{1,0:T(4,128)(2,1)S(1)} all-gather(bf16[3,256]{1,0:T(4,128)(2,1)S(1)} %copy-done.104), channel_id=1, replica_groups=mesh['wide'=8,'narrow'=4] {'narrow'}, dimensions={1}, use_global_device_ids=true | all-gather | bytes 7680 | tf_op jit(solution)/shard_map/all_gather | solution.py:582
  344.9 4.2 convolution_convert_fusion.16
  350.7 8.2 select_reduce_fusion.1
  358.9 8.7 fusion.8
  368.3 9.6 fusion.52
  380.5 6.4 fusion.36
  386.9 4.5 copy.101
  398.3 5.5 fusion.35
  407.1 16.7 %select_reduce_fusion = (f32[16,512]{1,0:T(8,128)S(1)}, f32[16,512,1176]{1,2,0:T(8,128)}) fusion(pred[512,1176]{0,1:T(8,128)(4,1)S(1)} %broadcast_compare_fusion, bf16[512,16,64]{0,2,1:T(8,128)(2,1)} %bitcast.312, bf16[1176,16,64]{0,2,1:T(8,128)(2,1)S(1)} %bitcast.305), kind=kOutput, calls=%fused_computation.21 | convolution fusion | flops 1252384768 | bytes 42627072 | tf_op jit(solution)/shard_map/while/body/eval_jaxpr/qhe,khe->hqk/dot_general | solution.py:502
  423.8 17.0 %fusion = f32[16,512]{1,0:T(8,128)S(1)} fusion(f32[16,512,1176]{1,2,0:T(8,128)} %get-tuple-element.291, f32[16,512]{1,0:T(8,128)S(1)} %get-tuple-element.290, pred[512,1176]{0,1:T(8,128)(4,1)S(1)} %broadcast_compare_fusion), kind=kLoop, calls=%fused_computation.19 | loop fusion | flops 28893184 | bytes 39202816 | tf_op jit(solution)/shard_map/while/body/eval_jaxpr/reduce_sum | solution.py:506
  441.5 17.3 %fusion.56 = bf16[16,64,512]{2,1,0:T(8,128)(2,1)} fusion(bf16[1176,16,64]{0,2,1:T(8,128)(2,1)S(1)} %bitcast.315, f32[16,512,1176]{1,2,0:T(8,128)} %get-tuple-element.291, f32[16,512]{1,0:T(8,128)S(1)} %fusion, f32[16,512]{1,0:T(8,128)S(1)} %get-tuple-element.290, pred[512,1176]{0,1:T(8,128)(4,1)S(1)} %broadcast_compare_fusion), kind=kOutput, calls=%fused_computation.143 | convolution fusion | flops 1272184832 | bytes 42659840 | tf_op jit(solution)/shard_map/while/body/eval_jaxpr/hqk,khe->qhe/dot_general | solution.py:508
  458.8 11.9 %all_gather.11 = bf16[4,1024]{1,0:T(4,128)(2,1)S(1)} all-gather(bf16[4,256]{1,0:T(4,128)(2,1)S(1)} %reshape.614), channel_id=1, replica_groups=mesh['wide'=8,'narrow'=4] {'narrow'}, dimensions={1}, use_global_device_ids=true | all-gather | bytes 10240 | tf_op jit(solution)/shard_map/all_gather | solution.py:584
  470.7 11.5 %copy.104 = bf16[1024,4,1024]{0,2,1:T(8,128)(2,1)} copy(bf16[1024,4,1024]{2,0,1:T(8,128)(2,1)} %bitcast.311) | data formatting | bytes 16777216 | tf_op jit(solution)/shard_map/transpose | solution.py:580
  486.6 31.0 %multiply_convert_fusion.2 = (bf16[512,4096]{1,0:T(8,128)(2,1)}, f32[512,4096]{1,0:T(8,128)}, f32[512,4096]{1,0:T(8,128)}) fusion(f32[4096]{0:T(1024)S(1)} %bitcast.402, bf16[1024,4096]{0,1:T(8,128)(2,1)S(1)} %bitcast.323, f32[512,1024]{1,0:T(8,128)S(1)} %get-tuple-element.293, f32[1024]{0:T(1024)S(1)} %bitcast.414, f32[1024]{0:T(1024)S(1)} %bitcast.405, ...), kind=kOutput, calls=%fused_computation.55 | convolution fusion | flops 4436000768 | bytes 31485952 | tf_op jit(solution)/shard_map/dot_general | solution.py:465
  517.5 12.3 %convert_reduce_fusion = (f32[4096]{0:T(1024)S(1)}, bf16[512,4096]{1,0:T(8,128)(2,1)}) fusion(f32[512,4096]{1,0:T(8,128)} %get-tuple-element.244, bf16[4096,1024]{1,0:T(8,128)(2,1)S(1)} %bitcast.331, bf16[1,512,1024]{2,1,0:T(8,128)(2,1)S(1)} %copy-done.60, f32[512,4096]{1,0:T(8,128)} %get-tuple-element.294, f32[4096]{0:T(1024)S(1)} %bitcast.403), kind=kOutput, calls=%fused_computation.53 | convolution fusion | flops 4330614784 | bytes 30441472 | tf_op jit(solution)/shard_map/rb,ab->ra/dot_general | solution.py:473
  529.9 7.4 multiply_reduce_fusion.2
  544.1 30.0 %multiply_reduce_fusion = (f32[16,512]{1,0:T(8,128)S(1)}, f32[16,512,1176]{1,2,0:T(8,128)}) fusion(f32[16,512,1176]{1,2,0:T(8,128)} %get-tuple-element.291, f32[16,512]{1,0:T(8,128)S(1)} %copy-done.69, pred[512,1176]{0,1:T(8,128)(4,1)S(1)} %broadcast_compare_fusion, bf16[512,16,64]{0,2,1:T(8,128)(2,1)} %bitcast.342, bf16[1176,16,64]{0,2,1:T(8,128)(2,1)S(1)} %bitcast.316), kind=kOutput, calls=%fused_computation.12 | convolution fusion | flops 1271652352 | bytes 81195008 | tf_op jit(solution)/shard_map/while/body/eval_jaxpr/qhe,khe->hqk/dot_general | solution.py:530
  574.1 31.7 %multiply_convert_fusion = bf16[16,512,1176]{1,2,0:T(8,128)(2,1)} fusion(f32[16,512,1176]{1,2,0:T(8,128)} %get-tuple-element.297, f32[16,512,1176]{1,2,0:T(8,128)} %get-tuple-element.291, f32[16,512]{1,0:T(8,128)S(1)} %get-tuple-element.296, f32[16,512]{1,0:T(8,128)S(1)} %copy-done.69, pred[512,1176]{0,1:T(8,128)(4,1)S(1)} %broadcast_compare_fusion), kind=kLoop, calls=%fused_computation.11 | loop fusion | flops 48168960 | bytes 97005568 | tf_op jit(solution)/shard_map/while/body/eval_jaxpr/convert_element_type | solution.py:534
  605.9 9.9 convert_reduce_fusion.4
  623.5 8.0 convert_reduce_fusion.5
  631.5 11.7 %multiply_reduce_fusion.1 = (f32[16,512]{1,0:T(8,128)S(1)}, f32[16,512,512]{1,2,0:T(8,128)}) fusion(f32[16,512,512]{1,2,0:T(8,128)} %get-tuple-element.287, f32[16,512]{1,0:T(8,128)S(1)} %copy-done.70, pred[512,512]{0,1:T(8,128)(4,1)S(1)} %copy-done.32, bf16[512,16,64]{0,2,1:T(8,128)(2,1)S(1)} %bitcast.347, bf16[512,16,64]{0,2,1:T(8,128)(2,1)S(1)} %bitcast.345), kind=kOutput, calls=%fused_computation.29 | convolution fusion | flops 553639936 | bytes 35979264 | tf_op jit(solution)/shard_map/while/body/eval_jaxpr/qhe,khe->hqk/dot_general | solution.py:530
  643.3 12.4 %multiply_convert_fusion.1 = bf16[16,512,512]{1,2,0:T(8,128)(2,1)S(1)} fusion(f32[16,512,512]{1,2,0:T(8,128)} %get-tuple-element.300, f32[16,512,512]{1,2,0:T(8,128)} %get-tuple-element.287, f32[16,512]{1,0:T(8,128)S(1)} %get-tuple-element.299, f32[16,512]{1,0:T(8,128)S(1)} %copy-done.70, pred[512,512]{0,1:T(8,128)(4,1)S(1)} %copy-done.32), kind=kLoop, calls=%fused_computation.28 | loop fusion | flops 20971520 | bytes 42270720 | tf_op jit(solution)/shard_map/while/body/eval_jaxpr/convert_element_type | solution.py:534
  670.3 18.2 %convert_reduce_fusion.1 = (f32[16,64]{1,0:T(8,128)S(1)}, bf16[16,64,1176]{2,1,0:T(8,128)(2,1)}) fusion(bf16[512,16,64]{0,2,1:T(8,128)(2,1)} %bitcast.343, f32[16,512,1176]{1,2,0:T(8,128)} %get-tuple-element.291, f32[16,512]{1,0:T(8,128)S(1)} %copy-done.69, pred[512,1176]{0,1:T(8,128)(4,1)S(1)} %broadcast_compare_fusion), kind=kOutput, calls=%fused_computation.74 | convolution fusion | flops 1265638400 | bytes 42631168 | tf_op jit(solution)/shard_map/while/body/eval_jaxpr/hqk,qhe->khe/dot_general | solution.py:524
  690.1 10.1 convolution_convert_fusion.2
  711.8 4.9 fusion.107
  716.7 6.1 convolution_convert_fusion.5
  729.1 5.4 convolution_convert_fusion.1
  734.5 7.1 convolution_convert_fusion
  741.7 10.3 fusion.57
  752.0 4.1 convolution_convert_fusion.4
  756.1 4.8 convolution_add_fusion
  788.3 190.7 %shard_map.196 = bf16[16,256,1024]{2,1,0:T(8,128)(2,1)} custom-call(bf16[16,4,256,1024]{3,2,1,0:T(8,128)(2,1)} %constant_dynamic-update-slice_fusion.grads_ref), custom_call_target="tpu_custom_call" | custom-call | tf_op jit(solution)/shard_map/pallas_call | solution.py:435
  979.1 7.1 fusion.98
  993.2 5.1 reshape.622
  998.3 8.3 copy.111
  1006.6 5.6 reshape.623
  1012.2 6.9 copy.110
  1019.1 5.8 reshape.624
  1026.8 24.3 %all-reduce = (f32[3,256]{1,0:T(4,128)}, f32[10,256]{1,0:T(8,128)}, f32[1024]{0:T(1024)}) all-reduce(f32[3,256]{1,0:T(4,128)S(1)} %copy.117, f32[10,256]{1,0:T(8,128)} %reduce-scatter.8.cloned.1.call-done, f32[1024]{0:T(1024)S(1)} %bitcast.404), channel_id=1, replica_groups=mesh['wide'=8,'narrow'=4] {'wide'}, use_global_device_ids=true, to_apply=%region_23.24 | all-reduce | flops 4352 | bytes 34816 | tf_op jit(solution)/shard_map/psum | solution.py:725
  (358 shorter events, 155.9 us)
Async XLA Ops:
  7.2 1017.7 %reduce-scatter.10.cloned.1.call-start = ((), (), s32[]{:S(2)}) async-start(), calls=%async_computation.4 | async-start | bytes 655360
  11.2 5.4 copy-start.59
  292.6 43.6 %copy-start.28 = (bf16[1,4,256,1024]{3,2,1,0:T(8,128)(2,1)}, bf16[1,4,256,1024]{3,2,1,0:T(8,128)(2,1)S(1)}, u32[]{:S(2)}) copy-start(bf16[1,4,256,1024]{3,2,1,0:T(8,128)(2,1)S(1)} %get-tuple-element.254) | copy-start | bytes 6291460
  292.7 48.5 %copy-start.44 = (bf16[1,4,256,1024]{3,2,1,0:T(8,128)(2,1)}, bf16[1,4,256,1024]{3,2,1,0:T(8,128)(2,1)S(1)}, u32[]{:S(2)}) copy-start(bf16[1,4,256,1024]{3,2,1,0:T(8,128)(2,1)S(1)} %get-tuple-element.253) | copy-start | bytes 6291460
  292.7 13.5 %copy-start.95 = (bf16[10,256]{1,0:T(8,128)(2,1)S(1)}, bf16[10,256]{1,0:T(8,128)(2,1)}, u32[]{:S(2)}) copy-start(bf16[10,256]{1,0:T(8,128)(2,1)} %param.21) | copy-start | bytes 15364
  292.7 30.3 %copy-start.104 = (bf16[3,256]{1,0:T(4,128)(2,1)S(1)}, bf16[3,256]{1,0:T(4,128)(2,1)}, u32[]{:S(2)}) copy-start(bf16[3,256]{1,0:T(4,128)(2,1)} %param.20) | copy-start | bytes 4612
  292.7 42.9 %copy-start.3 = (bf16[1,512,1024]{2,1,0:T(8,128)(2,1)S(1)}, bf16[1,512,1024]{2,1,0:T(8,128)(2,1)}, u32[]{:S(2)}) copy-start(bf16[1,512,1024]{2,1,0:T(8,128)(2,1)} %param.12) | copy-start | bytes 3145732
  322.9 22.0 %copy-start.101 = (f32[1,1024]{1,0:T(1,128)}, f32[1,1024]{1,0:T(1,128)S(1)}, u32[]{:S(2)}) copy-start(f32[1,1024]{1,0:T(1,128)S(1)} %get-tuple-element.281) | copy-start | bytes 12292
  322.9 72.5 %copy-start.99 = (f32[1,1024]{1,0:T(1,128)}, f32[1,1024]{1,0:T(1,128)S(1)}, u32[]{:S(2)}) copy-start(f32[1,1024]{1,0:T(1,128)S(1)} %get-tuple-element.276) | copy-start | bytes 12292
  335.6 9.3 copy-start.71
  335.6 59.9 %copy-start.89 = (f32[1,1024]{1,0:T(1,128)}, f32[1,1024]{1,0:T(1,128)S(1)}, u32[]{:S(2)}) copy-start(f32[1,1024]{1,0:T(1,128)S(1)} %get-tuple-element.284) | copy-start | bytes 12292
  335.8 9.1 copy-start.73
  336.3 8.7 copy-start.85
  336.3 4.6 copy-start.76
  341.1 27.2 %copy-start.31 = (pred[512,512]{0,1:T(8,128)(4,1)}, pred[512,512]{0,1:T(8,128)(4,1)S(1)}, u32[]{:S(2)}) copy-start(pred[512,512]{0,1:T(8,128)(4,1)S(1)} %fusion.64) | copy-start | bytes 786436
  344.9 5.8 copy-start.16
  350.7 8.2 copy-start.14
  358.9 9.4 copy-start.33
  368.3 9.6 copy-start.37
  386.9 4.5 copy-start.106
  386.9 4.6 copy-start.21
  406.7 17.1 %copy-start.1 = (bf16[1176,1024]{0,1:T(8,128)(2,1)}, bf16[1176,1024]{0,1:T(8,128)(2,1)S(1)}, u32[]{:S(2)}) copy-start(bf16[1176,1024]{0,1:T(8,128)(2,1)S(1)} %copy.103) | copy-start | bytes 7225348
  423.8 17.6 %copy-start.12 = (bf16[1176,1024]{0,1:T(8,128)(2,1)S(1)}, bf16[1176,1024]{0,1:T(8,128)(2,1)}, u32[]{:S(2)}) copy-start(bf16[1176,1024]{0,1:T(8,128)(2,1)} %copy.101) | copy-start | bytes 7225348
  441.5 17.4 %copy-start.105 = (bf16[1024]{0:T(1024)(128)(2,1)S(1)}, bf16[1024]{0:T(1024)(128)(2,1)}, u32[]{:S(2)}) copy-start(bf16[1024]{0:T(1024)(128)(2,1)} %param.22) | copy-start | bytes 6148
  470.7 11.5 %copy-start.7 = (f32[512,1024]{1,0:T(8,128)S(1)}, f32[512,1024]{1,0:T(8,128)}, u32[]{:S(2)}) copy-start(f32[512,1024]{1,0:T(8,128)} %copy-done.6) | copy-start | bytes 6291460
  470.7 11.5 %copy-start.103 = (f32[1,1024]{1,0:T(1,128)S(1)}, f32[1,1024]{1,0:T(1,128)}, u32[]{:S(2)}) copy-start(f32[1,1024]{1,0:T(1,128)} %get-tuple-element.275) | copy-start | bytes 12292
  470.7 15.3 %copy-start.87 = (f32[1,1024]{1,0:T(1,128)S(1)}, f32[1,1024]{1,0:T(1,128)}, u32[]{:S(2)}) copy-start(f32[1,1024]{1,0:T(1,128)} %get-tuple-element.283) | copy-start | bytes 12292
  470.7 15.3 %copy-start.97 = (f32[1,1024]{1,0:T(1,128)S(1)}, f32[1,1024]{1,0:T(1,128)}, u32[]{:S(2)}) copy-start(f32[1,1024]{1,0:T(1,128)} %get-tuple-element.274) | copy-start | bytes 12292
  482.2 4.3 copy-start.23
  482.2 35.3 %slice-start = ((s8[8388608]{0:T(1024)(128)(4,1)}), s8[4194304]{0:T(1024)(128)(4,1)S(1)}, s32[]{:S(2)}) async-start(s8[8388608]{0:T(1024)(128)(4,1)} %bitcast.329), calls=%async_computation.6 | async-start | bytes 8388608
  485.7 51.6 %copy-start.26 = (f32[512,1024]{1,0:T(8,128)}, f32[512,1024]{1,0:T(8,128)S(1)}, u32[]{:S(2)}) copy-start(f32[512,1024]{1,0:T(8,128)S(1)} %get-tuple-element.293) | copy-start | bytes 6291460
  485.7 51.6 %copy-start.81 = (f32[512]{0:T(512)}, f32[512]{0:T(512)S(1)}, u32[]{:S(2)}) copy-start(f32[512]{0:T(512)S(1)} %broadcast_multiply_fusion) | copy-start | bytes 6148
  486.0 51.3 %copy-start.93 = (f32[512]{0:T(512)}, f32[512]{0:T(512)S(1)}, u32[]{:S(2)}) copy-start(f32[512]{0:T(512)S(1)} %fusion.74) | copy-start | bytes 6148
  486.6 31.0 %slice-start.1 = ((s8[8388608]{0:T(1024)(128)(4,1)}), s8[4194304]{0:T(1024)(128)(4,1)S(1)}, s32[]{:S(2)}) async-start(s8[8388608]{0:T(1024)(128)(4,1)} %bitcast.329), calls=%async_computation.7 | async-start | bytes 8388608
  486.6 31.0 %copy-start.60 = (bf16[1,512,1024]{2,1,0:T(8,128)(2,1)S(1)}, bf16[1,512,1024]{2,1,0:T(8,128)(2,1)}, u32[]{:S(2)}) copy-start(bf16[1,512,1024]{2,1,0:T(8,128)(2,1)} %param.23) | copy-start | bytes 3145732
  539.5 4.6 copy-start.13
  539.5 4.6 copy-start.69
  574.1 31.7 %copy-start.2 = (bf16[1176,1024]{0,1:T(8,128)(2,1)S(1)}, bf16[1176,1024]{0,1:T(8,128)(2,1)}, u32[]{:S(2)}) copy-start(bf16[1176,1024]{0,1:T(8,128)(2,1)} %copy-done.1) | copy-start | bytes 7225348
  605.8 9.9 copy-start.8
  605.8 9.9 copy-start.47
  605.8 9.9 copy-start.80
  605.9 9.9 copy-start.90
  605.9 9.9 copy-start.92
  623.5 8.1 copy-start.34
  631.5 31.6 %copy-start.67 = (bf16[16,64,512]{2,1,0:T(8,128)(2,1)}, bf16[16,64,512]{2,1,0:T(8,128)(2,1)S(1)}, u32[]{:S(2)}) copy-start(bf16[16,64,512]{2,1,0:T(8,128)(2,1)S(1)} %get-tuple-element.305) | copy-start | bytes 3145732
  643.3 12.4 %copy-start.15 = (bf16[512,1024]{0,1:T(8,128)(2,1)S(1)}, bf16[512,1024]{0,1:T(8,128)(2,1)}, u32[]{:S(2)}) copy-start(bf16[512,1024]{0,1:T(8,128)(2,1)} %copy-done.14) | copy-start | bytes 3145732
  669.1 356.7 %reduce-scatter.12.cloned.1.call-start = ((), (), s32[]{:S(2)}) async-start(), calls=%async_computation.5 | async-start | bytes 655360
  670.3 19.8 %copy-start.5 = (bf16[512,1024]{0,1:T(8,128)(2,1)S(1)}, bf16[512,1024]{0,1:T(8,128)(2,1)}, u32[]{:S(2)}) copy-start(bf16[512,1024]{0,1:T(8,128)(2,1)} %copy.102) | copy-start | bytes 3145732
  670.3 356.6 %reduce-scatter.8.cloned.1.call-start = ((), (), s32[]{:S(2)}) async-start(), calls=%async_computation.3 | async-start | bytes 81920 | tf_op jit(solution)/shard_map/reduce_scatter | solution.py:722
  690.1 10.1 copy-start.36
  690.1 10.1 copy-start.102
  700.2 11.6 %copy-start.30 = (bf16[16,64,1176]{2,1,0:T(8,128)(2,1)}, bf16[16,64,1176]{2,1,0:T(8,128)(2,1)S(1)}, u32[]{:S(2)}) copy-start(bf16[16,64,1176]{2,1,0:T(8,128)(2,1)S(1)} %convolution_convert_fusion.2) | copy-start | bytes 7225348
  711.8 4.9 copy-start.39
  716.7 6.1 copy-start.25
  716.7 6.1 copy-start.66
  734.5 7.2 copy-start.96
  734.5 21.6 %slice-start.2 = ((s8[4816896]{0:T(1024)(128)(4,1)}), s8[622592]{0:T(1024)(128)(4,1)S(1)}, s32[]{:S(2)}) async-start(s8[4816896]{0:T(1024)(128)(4,1)} %bitcast.438), calls=%async_computation.8 | async-start | bytes 1245184
  741.7 10.3 copy-start.40
  741.7 10.3 copy-start.107
  741.7 14.4 %slice-start.3 = ((s8[4816896]{0:T(1024)(128)(4,1)}), s8[4194304]{0:T(1024)(128)(4,1)S(1)}, s32[]{:S(2)}) async-start(s8[4816896]{0:T(1024)(128)(4,1)} %bitcast.438), calls=%async_computation.9 | async-start | bytes 8388608
  752.0 4.2 copy-start.41
  756.1 4.8 copy-start.55
  979.0 7.1 copy-start.11
  979.1 9.1 copy-start
  (53 other events, 125.2 us)
Sparse Core Ops, SparseCore 0:
  669.2 19.6 reduce-scatter.9
  691.2 19.8 reduce-scatter.11
  713.3 17.2 reduce-scatter.7
